TPU v7x, 32 devices: a whole 2x2x4 slice. The times are simulated.
32 devices in a mesh: sec: 4 (over z), dom: 8 (over y, x, core).
Axes of the slice: x: 2, y: 2, z: 4, core: 2. Of those that a mesh axis runs over, the one named last changes fastest.
Arguments:
- rhs: float32 [256, 2048], P(('sec', 'dom')), may hold values from -6 to 6
- fine_blocks: float32 [256, 8, 4096], P(('sec', 'dom')), may hold values from -1 to 3
- fine_columns: int32 [256, 8], P(('sec', 'dom')), may hold values from 0 to 39, as said below
- send_lists: int32 [32, 4, 8], P(('sec', 'dom')), may hold values from -1 to 7, as said below
- smoother: bfloat16 [256, 4096], P(('sec', 'dom')), may hold values from -1 to 1
- prolong: bfloat16 [256, 384], P(('sec', 'dom')), may hold values from -4.1875 to 4.1875
- agg_map: int32 [256], P(('sec', 'dom')), may hold values from 0 to 1, as said below
- coarse_blocks: float32 [64, 8, 36], P(('sec', 'dom')), may hold values from -2 to 4
- coarse_columns: int32 [64, 8], P(('sec', 'dom')), may hold values from 0 to 63, as said below
- coarse_smoother: float32 [64, 36], P(('sec', 'dom')), may hold values from -1 to 1.5
Outputs:
- solution: float32 [256, 2048], P(('sec', 'dom'))
- coarse_solution: float32 [64, 192], P(('sec', 'dom'))
Inputs may be any that keep to these rules, and one draw needn't show every extreme that they name: `fine_columns`: slot 0 of a row names the row itself; the other slots name own rows or halo rows of the extended array. `send_lists`: each entry is a block row of the sender or -1 for an empty slot; empty slots come last and every list has at least 4 filled slots. `agg_map`: every aggregate of a device holds at least one of its block rows. `coarse_columns`: slot 0 of a row names the row itself. Slots 1, 2, 3, 4 name an aggregate of device (s, d-1), (s, d+1), (s-1, d), (s+1, d) respectively, where (s, d) is the row's device, or the row itself where that device does not exist. The other slots may name any aggregate.
All inputs are finite; a program needn't handle non-finite values.
Results may differ from a plain program's by a relative error of at most 0.012.
Values sent between devices are 32-bit elements; how exact they have to be, the bound alone decides.
A program may use at most 128 MiB of HBM per device.

v0:
```python
import functools

import jax
import jax.numpy as jnp
from jax import lax
from jax.experimental import pallas as pl
from jax.experimental.pallas import tpu as pltpu
from jax.sharding import PartitionSpec as P

B = 64
R = 32
BC = 6
K = 8
KC = 8
NPRE = 5
NPOST = 5
CITERS = 4
NAGG = 2
HALF = 4 * B
TURNS = NPRE + NPOST
MESH = pl.DeviceIdType.MESH
DENSE_LIMIT = 1024


def split2(value):
    high = value.astype(jnp.bfloat16)
    return high, (value - high.astype(jnp.float32)).astype(jnp.bfloat16)


def cycle_kernel(
    n_sec, n_dom,
    rhs, fine, smooth, restrict, prolong, coarse_own, lists_own, columns, agg,
    x_out, w_out,
    a_high, a_low, fields, halo, turned, gathered, slots,
    lists_in, lists_scalar, tiles_in, tiles3, dense, dense_high, dense_low, inverse,
    coarse_in, state,
    halo_send, halo_recv, list_send, list_recv, list_local,
    tile_send, tile_recv, coarse_send, coarse_recv,
):
    count = n_sec * n_dom
    rows = 8 * count
    s, d = lax.axis_index("sec"), lax.axis_index("dom")
    me = s * n_dom + d
    links = (
        ((s, d + 1), d < n_dom - 1, d > 0),
        ((s, d - 1), d > 0, d < n_dom - 1),
        ((s + 1, d), s < n_sec - 1, s > 0),
        ((s - 1, d), s > 0, s < n_sec - 1),
    )
    lane = lax.broadcasted_iota(jnp.int32, (1, 128), 1)
    group = lane // R

    def to_others(action):
        def visit(step, carry):
            other = lax.rem(me + step, count)
            action((other // n_dom, lax.rem(other, n_dom)))
            return carry

        lax.fori_loop(1, count, visit, 0)

    barrier = pltpu.get_barrier_semaphore()
    to_others(lambda where: pl.semaphore_signal(barrier, inc=1, device_id=where, device_id_type=MESH))

    def diagonal(product):
        parts = [product[g * B:(g + 1) * B] for g in range(4)]
        return jnp.where(group == 0, parts[0], jnp.where(group == 1, parts[1], jnp.where(group == 2, parts[2], parts[3])))

    def relax(half, value):
        product = jnp.dot(
            smooth[half * HALF:(half + 1) * HALF, :], value.astype(jnp.bfloat16), preferred_element_type=jnp.float32
        )
        return diagonal(product)

    def halo_copy(turn, q):
        return pltpu.make_async_remote_copy(
            src_ref=fields.at[turn], dst_ref=halo.at[turn, q],
            send_sem=halo_send.at[turn, q], recv_sem=halo_recv.at[turn, q],
            device_id=links[q][0], device_id_type=MESH,
        )

    def list_copy(q):
        return pltpu.make_async_remote_copy(
            src_ref=lists_own, dst_ref=lists_in.at[q],
            send_sem=list_send.at[q], recv_sem=list_recv.at[q],
            device_id=links[q][0], device_id_type=MESH,
        )

    def turn_tiles(value, source):
        for half in range(2):
            part = value[half * B:(half + 1) * B, :]
            for step in range(4):
                turned[(source * 2 + half) * 4 + step] = part if step == 0 else pltpu.roll(part, step * R, 1)

    def start_halo(turn):
        for q in range(4):
            @pl.when(links[q][1])
            def _():
                halo_copy(turn, q).start()

    def publish(turn, halves):
        for half in range(2):
            fields[turn, half * B:(half + 1) * B, :] = halves[half]
        start_halo(turn)
        turn_tiles(fields[turn], 0)

    def spread_copy(source, place, send_sem, recv_sem, where):
        return pltpu.make_async_remote_copy(
            src_ref=source, dst_ref=place.at[me], send_sem=send_sem, recv_sem=recv_sem,
            device_id=where, device_id_type=MESH,
        )

    def wait_bytes(place, sem):
        part = place.at[pl.ds(0, count - 1)]
        pltpu.make_async_copy(part, part, sem).wait()

    first = [relax(half, rhs[half * B:(half + 1) * B, :]) for half in range(2)]
    high, low = split2(fine[...])
    a_high[...] = high
    a_low[...] = low
    dense[...] = jnp.zeros_like(dense)
    turned[40:44] = jnp.zeros((4, B, 128), jnp.float32)
    for q in range(4):
        @pl.when(jnp.logical_not(links[q][2]))
        def _():
            lists_in[q] = jnp.full((8, 128), -1, jnp.int32)

    pl.semaphore_wait(barrier, count - 1)
    for q in range(4):
        @pl.when(links[q][1])
        def _():
            list_copy(q).start()
    publish(0, first)
    tiles_in[me] = coarse_own[...]
    to_others(lambda where: spread_copy(coarse_own, tiles_in, tile_send, tile_recv, where).start())
    for q in range(4):
        @pl.when(links[q][2])
        def _():
            list_copy(q).wait_recv()
    to_scalar = pltpu.make_async_copy(lists_in, lists_scalar, list_local)
    to_scalar.start()
    to_scalar.wait()

    def find_slot(index, carry):
        column = columns[index]
        row = index // K
        q = jnp.maximum(column // 8 - 1, 0)
        listed = lists_scalar[q, q, lax.rem(column, 8)]
        place = jnp.where(column < 8, column, jnp.where(listed < 0, 40, (q + 1) * 8 + listed))
        piece = jnp.where(place >= 40, 10, place // 4)
        slots[index] = piece * 4 + lax.rem(row - place + 64, 4)
        return carry

    lax.fori_loop(0, 8 * K, find_slot, 0)

    def residual(turn):
        for q in range(4):
            @pl.when(links[q][2])
            def _():
                halo_copy(turn, q).wait_recv()
                turn_tiles(halo[turn, q], q + 1)
        result = []
        for half in range(2):
            for k in range(K):
                t = [turned[slots[(half * 4 + g) * K + k]] for g in range(4)]
                tile = jnp.where(group == 0, t[0], jnp.where(group == 1, t[1], jnp.where(group == 2, t[2], t[3])))
                high, low = split2(tile)
                gathered[half, k * B:(k + 1) * B, 0:128] = high
                gathered[half, k * B:(k + 1) * B, 128:256] = low
            span = slice(half * HALF, (half + 1) * HALF)
            both = jnp.dot(a_high[span, :], gathered[half], preferred_element_type=jnp.float32)
            rest = jnp.dot(a_low[span, :], gathered[half, :, 0:128], preferred_element_type=jnp.float32)
            product = both[:, 0:128] + both[:, 128:256] + rest
            result.append(rhs[half * B:(half + 1) * B, :] - diagonal(product))
        return result

    def sweep(turn):
        left = residual(turn)
        return [fields[turn, half * B:(half + 1) * B, :] + relax(half, left[half]) for half in range(2)]

    position = lax.broadcasted_iota(jnp.int32, (1, 2 * rows), 1)
    within = lax.rem(position, rows)
    named = jnp.where(lax.rem(position, 8) < BC, (within // 8 * NAGG + position // rows).astype(jnp.float32), -1.0)
    from_lane = lax.rem(lax.broadcasted_iota(jnp.int32, (384, 128), 0), 128)
    to_lane = lax.broadcasted_iota(jnp.int32, (384, 128), 1)

    def pick(wanted):
        chosen = (from_lane == wanted).astype(jnp.float32).astype(jnp.bfloat16)
        return jnp.dot(tiles3[...], chosen, preferred_element_type=jnp.float32)

    def add_blocks(k):
        for a in range(NAGG):
            spread = pick((a * KC + k) * 8 + lax.rem(to_lane, 8))
            names = jnp.broadcast_to(spread.reshape(count, 8, 128)[:, BC:BC + 1, :], (count, 8, 128)).reshape(rows, 128)
            for v in range(2 * rows // 128):
                cut = slice(v * 128, (v + 1) * 128)
                dense[a * rows:(a + 1) * rows, cut] += jnp.where(names == named[:, cut], spread, 0.0)

    def pre_turn(turn, carry):
        publish(turn + 1, sweep(turn))

        @pl.when(turn == 0)
        def _():
            wait_bytes(tiles_in, tile_recv)
            whole = tiles_in[...].reshape(rows, 128)
            high, low = split2(whole)
            tiles3[:, 0:128] = high
            tiles3[:, 128:256] = low
            tiles3[:, 256:384] = (whole - high.astype(jnp.float32) - low.astype(jnp.float32)).astype(jnp.bfloat16)

        add_blocks(2 * turn)
        add_blocks(2 * turn + 1)
        return carry

    lax.fori_loop(0, NPRE - 1, pre_turn, 0)
    for j in range(BC):
        inverse[j] = pick((to_lane // R * KC + j) * 8 + BC)

    left = residual(NPRE - 1)
    sums = [jnp.zeros((8, 128), jnp.float32) for _ in range(NAGG)]
    for half in range(2):
        terms = jnp.dot(
            restrict[half * 32:(half + 1) * 32, :], left[half].astype(jnp.bfloat16), preferred_element_type=jnp.float32
        )
        for g in range(4):
            kept = jnp.where(group == g, terms[g * 8:(g + 1) * 8], 0.0)
            for a in range(NAGG):
                sums[a] = sums[a] + jnp.where(agg[half * 4 + g] == a, kept, 0.0)

    def fold(value):
        value = value + pltpu.roll(value, 64, 1)
        return value + pltpu.roll(value, 32, 1)

    folded = [fold(value) for value in sums]
    coarse_in[me] = jnp.where(group == 0, folded[0], jnp.where(group == 1, folded[1], 0.0))
    to_others(lambda where: spread_copy(coarse_in.at[me], coarse_in, coarse_send, coarse_recv, where).start())
    high, low = split2(dense[...])
    dense_high[...] = high
    dense_low[...] = low
    wait_bytes(coarse_in, coarse_recv)
    right = coarse_in[...].reshape(rows, 128)

    def precond(value):
        tiles = value.reshape(count, 8, 128)
        total = jnp.zeros((rows, 128), jnp.float32)
        for j in range(BC):
            total = total + inverse[j] * jnp.broadcast_to(tiles[:, j:j + 1, :], (count, 8, 128)).reshape(rows, 128)
        return total

    def coarse_turn(step, carry):
        value = state[...]
        value_r, value_l = pltpu.roll(value, R, 1), pltpu.roll(value, 128 - R, 1)
        stacked = jnp.concatenate(
            [jnp.where(group == 0, value, value_r), jnp.where(group == 0, value_l, value)], axis=0
        )
        high, low = split2(stacked)
        both = jnp.dot(dense_high[...], jnp.concatenate([high, low], axis=1), preferred_element_type=jnp.float32)
        rest = jnp.dot(dense_low[...], high, preferred_element_type=jnp.float32)
        product = both[:, 0:128] + both[:, 128:256] + rest
        applied = jnp.where(group == 0, product[0:rows], product[rows:2 * rows])
        inside = lax.rem(lax.broadcasted_iota(jnp.int32, (rows, 1), 0), 8) < BC
        state[...] = value + precond(jnp.where(inside & (group < NAGG), right - applied, 0.0))
        return carry

    state[...] = precond(right)
    lax.fori_loop(0, CITERS, coarse_turn, 0)
    own = state[pl.ds(pl.multiple_of(me * 8, 8), 8), :]
    w_out[...] = own
    answers = [
        fold(jnp.where(group == a, own, 0.0)) for a in range(NAGG)
    ]
    corrected = []
    for half in range(2):
        picked = jnp.zeros((8, 128), jnp.float32)
        for g in range(4):
            for a in range(NAGG):
                picked = picked + jnp.where((group == g) & (agg[half * 4 + g] == a), answers[a], 0.0)
        product = jnp.dot(
            prolong[half * HALF:(half + 1) * HALF, :], picked,
            precision=lax.Precision.HIGHEST, preferred_element_type=jnp.float32,
        )
        corrected.append(fields[NPRE - 1, half * B:(half + 1) * B, :] + diagonal(product))
    publish(NPRE, corrected)

    def post_turn(turn, carry):
        publish(turn + 1, sweep(turn))
        return carry

    lax.fori_loop(NPRE, TURNS - 1, post_turn, 0)
    last = sweep(TURNS - 1)
    for half in range(2):
        x_out[half * B:(half + 1) * B, :] = last[half]

    def drain(turn, carry):
        for q in range(4):
            @pl.when(links[q][1])
            def _():
                halo_copy(turn, q).wait_send()
        return carry

    lax.fori_loop(0, TURNS, drain, 0)
    for q in range(4):
        @pl.when(links[q][1])
        def _():
            list_copy(q).wait_send()
    wait_bytes(tiles_in, tile_send)
    wait_bytes(coarse_in, coarse_send)


def fused_cycle(n_sec, n_dom, rhs, fine_blocks, fine_columns, send_lists, smoother, prolong, agg_map,
                coarse_blocks, coarse_columns, coarse_smoother):
    count = n_sec * n_dom
    rows = 8 * count
    packed = rhs.reshape(2, 4, B, R).transpose(0, 2, 1, 3).reshape(2 * B, 4 * R)
    fine = fine_blocks.reshape(8, K, B, B).transpose(0, 2, 1, 3).reshape(8 * B, K * B)
    smooth = smoother.reshape(8 * B, B)
    tiles = jnp.pad(prolong.reshape(8, B, BC), ((0, 0), (0, 0), (0, 2)))
    restrict = tiles.transpose(0, 2, 1).reshape(64, B)
    lifts = tiles.reshape(8 * B, 8).astype(jnp.float32)
    lists = jnp.pad(send_lists[0], ((0, 4), (0, 120)), constant_values=-1)
    blocks = coarse_blocks.reshape(NAGG, KC, BC, BC)
    inverse = jnp.pad(coarse_smoother.reshape(NAGG, BC, BC).transpose(0, 2, 1), ((0, 0), (0, KC - BC), (0, 0)))
    upper = jnp.concatenate([blocks, inverse[..., None], jnp.zeros_like(inverse)[..., None]], axis=3)
    names = jnp.broadcast_to(coarse_columns.astype(jnp.float32)[:, :, None, None], (NAGG, KC, 1, BC))
    lower = jnp.pad(names, ((0, 0), (0, 0), (0, 1), (0, 2)))
    coarse_own = jnp.concatenate([upper, lower], axis=2).transpose(2, 0, 1, 3).reshape(8, 128)

    vmem = pl.BlockSpec(memory_space=pltpu.VMEM)
    smem = pl.BlockSpec(memory_space=pltpu.SMEM)
    f32, bf16 = jnp.float32, jnp.bfloat16
    x, w = pl.pallas_call(
        functools.partial(cycle_kernel, n_sec, n_dom),
        out_shape=(jax.ShapeDtypeStruct((2 * B, 128), f32), jax.ShapeDtypeStruct((8, 128), f32)),
        in_specs=[vmem] * 7 + [smem] * 2,
        out_specs=(vmem, vmem),
        scratch_shapes=[
            pltpu.VMEM((512, 512), bf16),
            pltpu.VMEM((512, 512), bf16),
            pltpu.VMEM((TURNS, 128, 128), f32),
            pltpu.VMEM((TURNS, 4, 128, 128), f32),
            pltpu.VMEM((44, B, 128), f32),
            pltpu.VMEM((2, 512, 256), bf16),
            pltpu.SMEM((64,), jnp.int32),
            pltpu.VMEM((4, 8, 128), jnp.int32),
            pltpu.SMEM((4, 8, 128), jnp.int32),
            pltpu.VMEM((count, 8, 128), f32),
            pltpu.VMEM((rows, 384), bf16),
            pltpu.VMEM((2 * rows, 2 * rows), f32),
            pltpu.VMEM((2 * rows, 2 * rows), bf16),
            pltpu.VMEM((2 * rows, 2 * rows), bf16),
            pltpu.VMEM((BC, rows, 128), f32),
            pltpu.VMEM((count, 8, 128), f32),
            pltpu.VMEM((rows, 128), f32),
            pltpu.SemaphoreType.DMA((TURNS, 4)),
            pltpu.SemaphoreType.DMA((TURNS, 4)),
            pltpu.SemaphoreType.DMA((4,)),
            pltpu.SemaphoreType.DMA((4,)),
            pltpu.SemaphoreType.DMA,
            pltpu.SemaphoreType.DMA,
            pltpu.SemaphoreType.DMA,
            pltpu.SemaphoreType.DMA,
            pltpu.SemaphoreType.DMA,
        ],
        compiler_params=pltpu.CompilerParams(
            collective_id=0, has_side_effects=True, vmem_limit_bytes=48 * 1024 * 1024
        ),
    )(packed, fine, smooth, restrict, lifts, coarse_own, lists, fine_columns.reshape(64), agg_map)
    solved = x.reshape(2, B, 4, R).transpose(0, 2, 1, 3).reshape(8, B * R)
    coarse = w[:BC, :NAGG * R].reshape(BC, NAGG, R).transpose(1, 0, 2).reshape(NAGG, BC * R)
    return solved, coarse


def passed_along(block, axis, distance):
    devices = range(lax.axis_size(axis))
    route = [(i - distance, i) for i in devices if i - distance in devices]
    return lax.ppermute(block, axis, route)


def coarse_terms(coarse_mats, where_col, piece):
    row_total = coarse_mats.shape[0]
    piece_rows = piece.shape[0]
    inside = (where_col >= 0) & (where_col < piece_rows)
    fetched = jnp.where(inside[..., None], piece[jnp.clip(where_col, 0, piece_rows - 1)], 0.0)
    fetched = fetched.reshape(row_total, KC, BC, R)
    return jnp.einsum(
        "nkij,nkjr->nir", coarse_mats, fetched, precision=lax.Precision.HIGHEST
    ).reshape(row_total, BC * R)


def coarse_solve(coarse_rhs, blocks, smooth_rows, fold_call):
    row_total = coarse_rhs.shape[0]
    coarse_mats = blocks.reshape(row_total, KC, BC, BC)
    inverse = smooth_rows.reshape(row_total, BC, BC)

    def precond(field):
        return jnp.einsum(
            "nij,njr->nir",
            inverse,
            field.reshape(row_total, BC, R),
            precision=lax.Precision.HIGHEST,
        ).reshape(row_total, BC * R)

    answer = precond(coarse_rhs)
    for repeat in range(CITERS):
        applied = fold_call(answer, coarse_mats)
        answer = answer + precond(coarse_rhs - applied)
    return answer


def staged_cycle(
    rhs,
    fine_blocks,
    fine_columns,
    send_lists,
    smoother,
    prolong,
    agg_map,
    coarse_blocks,
    coarse_columns,
    coarse_smoother,
):
    row_count = rhs.shape[0]
    lists = send_lists[0]
    chosen = jnp.clip(lists, 0, row_count - 1)
    present = (lists >= 0)[..., None]
    matrix_tiles = fine_blocks.reshape(row_count, K, B, B)
    smooth_tiles = smoother.reshape(row_count, B, B)
    prolong_tiles = prolong.reshape(row_count, B, BC)

    def apply_fine(vector):
        outgoing = jnp.where(present, vector[chosen], jnp.zeros((), vector.dtype))
        lower_dom = passed_along(outgoing[0], "dom", 1)
        upper_dom = passed_along(outgoing[1], "dom", -1)
        lower_sec = passed_along(outgoing[2], "sec", 1)
        upper_sec = passed_along(outgoing[3], "sec", -1)
        extended = jnp.concatenate([vector, lower_dom, upper_dom, lower_sec, upper_sec], axis=0)
        picked = extended[fine_columns].reshape(row_count, K, B, R)
        return jnp.einsum(
            "nkbc,nkcr->nbr", matrix_tiles, picked, precision=lax.Precision.HIGHEST
        ).reshape(row_count, B * R)

    def relax(vector):
        return jnp.einsum(
            "nbc,ncr->nbr",
            smooth_tiles,
            vector.reshape(row_count, B, R),
            preferred_element_type=jnp.float32,
        ).reshape(row_count, B * R)

    def sweep(iterate):
        residual = rhs - apply_fine(iterate)
        return iterate + relax(residual.astype(jnp.bfloat16))

    iterate = relax(rhs.astype(jnp.bfloat16))
    for repeat in range(NPRE - 1):
        iterate = sweep(iterate)
    residual = rhs - apply_fine(iterate)
    members = agg_map[:, None] == jnp.arange(NAGG, dtype=jnp.int32)[None, :]
    local_terms = jnp.einsum(
        "nbj,nbr->njr",
        prolong_tiles,
        residual.astype(jnp.bfloat16).reshape(row_count, B, R),
        preferred_element_type=jnp.float32,
    ).reshape(row_count, BC * R)
    coarse_rhs = jnp.dot(
        members.astype(jnp.float32).T, local_terms, precision=lax.Precision.HIGHEST
    )
    rhs_all, blocks_all, smooth_all = (
        lax.all_gather(coarse_rhs, "sec", axis=0, tiled=True),
        lax.all_gather(coarse_blocks, "sec", axis=0, tiled=True),
        lax.all_gather(coarse_smoother, "sec", axis=0, tiled=True),
    )
    columns_all = lax.all_gather(coarse_columns, "sec", axis=0, tiled=True)
    spread = lax.axis_size("dom")
    depth = lax.axis_size("sec")
    where_col = (
        columns_all // NAGG % spread * (depth * NAGG)
        + columns_all // (spread * NAGG) * NAGG
        + columns_all % NAGG
    )

    def fold_section(vector, coarse_mats):
        return coarse_terms(
            coarse_mats, where_col, lax.all_gather(vector, "dom", axis=0, tiled=True)
        )

    gathered_answer = coarse_solve(rhs_all, blocks_all, smooth_all, fold_section)
    own_answer = lax.dynamic_slice_in_dim(gathered_answer, lax.axis_index("sec") * NAGG, NAGG, 0)
    selected = jnp.dot(members.astype(jnp.float32), own_answer, precision=lax.Precision.HIGHEST)
    correction = jnp.einsum(
        "nbj,njr->nbr",
        prolong_tiles.astype(jnp.float32),
        selected.reshape(row_count, BC, R),
        precision=lax.Precision.HIGHEST,
    ).reshape(row_count, B * R)
    iterate = iterate + correction
    for repeat in range(NPOST):
        iterate = sweep(iterate)
    return (iterate, own_answer)


def solution(mesh):
    placed = (
        P(("sec", "dom"), None),
        P(("sec", "dom"), None, None),
        P(("sec", "dom"), None),
        P(("sec", "dom"), None, None),
        P(("sec", "dom"), None),
        P(("sec", "dom"), None),
        P(("sec", "dom")),
        P(("sec", "dom"), None, None),
        P(("sec", "dom"), None),
        P(("sec", "dom"), None),
    )
    n_sec, n_dom = mesh.shape["sec"], mesh.shape["dom"]
    fits = 2 * 8 * n_sec * n_dom <= DENSE_LIMIT
    local = functools.partial(fused_cycle, n_sec, n_dom) if fits else staged_cycle
    return jax.shard_map(
        local,
        mesh=mesh,
        in_specs=placed,
        out_specs=(P(("sec", "dom"), None), P(("sec", "dom"), None)),
        check_vma=False,
    )
```

profile of v0, /device:TPU:0, one launch (start us, length us, event | category | flops | bytes accessed | tf_op | source)
XLA Modules:
  0.0 74.5 jit_solution(147566252393050532)
XLA Ops:
  0.6 1.0 %reshape.55 = f32[2,4,64,32]{3,2,1,0:T(8,128)S(1)} reshape(f32[8,2048]{1,0:T(8,128)} %param.10) | data formatting | bytes 131072 | tf_op jit(solution)/shard_map/reshape | solution.py:313
  1.6 0.1 copy.20
  1.7 0.1 reshape.56
  1.9 0.1 copy.26.rhs
  1.9 3.1 %reshape.57 = f32[8,8,64,64]{3,2,1,0:T(8,128)} reshape(f32[8,8,4096]{2,1,0:T(8,128)} %param.11) | data formatting | bytes 2097152 | tf_op jit(solution)/shard_map/reshape | solution.py:314
  5.1 2.8 %copy.34 = f32[8,8,64,64]{3,1,2,0:T(8,128)S(1)} copy(f32[8,8,64,64]{3,2,1,0:T(8,128)} %reshape.57) | data formatting | bytes 2097152 | tf_op jit(solution)/shard_map/reshape | solution.py:314
  8.0 0.5 reshape.58.fine
  8.4 0.2 copy-done.1
  8.7 0.2 reshape.59.smooth
  8.9 0.2 reshape.60
  9.2 0.1 copy.22
  9.4 0.1 reshape.63
  9.5 0.2 copy.24
  9.7 0.1 reshape.62
  9.9 0.1 fusion
  10.0 0.1 reshape.64.coarse_own
  10.1 0.1 reshape.65.columns
  10.2 62.4 %shard_map.113 = (f32[128,128]{1,0:T(8,128)S(1)}, f32[8,128]{1,0:T(8,128)S(1)}) custom-call(f32[128,128]{1,0:T(8,128)S(1)} %copy.26.rhs, f32[512,512]{1,0:T(8,128)S(1)} %reshape.58.fine, bf16[512,64]{1,0:T(8,128)(2,1)S(1)} %reshape.59.smooth, bf16[64,64]{1,0:T(8,128)(2,1)S(1)} %bitcast.31, f32[512,8]{1,0:T(8,128)S(1)} %bitcast_convert_fusion.prolong, ...), custom_call_target="tpu_custom_call" | custom-call | tf_op jit(solution)/shard_map/pallas_call | solution.py:330
  72.6 0.1 copy.27
  72.7 0.1 reshape.66
  72.8 0.1 copy.28
  72.9 0.8 %reshape.67 = f32[8,2048]{1,0:T(8,128)} reshape(f32[2,4,64,32]{3,2,1,0:T(8,128)S(1)} %copy.28) | data formatting | bytes 131072 | tf_op jit(solution)/shard_map/reshape | solution.py:367
  73.7 0.1 reshape.68
  73.8 0.7 reshape.69
  (25 shorter events, 0.3 us)
Async XLA Ops:
  7.9 0.8 %copy-start.1 = (bf16[8,4096]{1,0:T(8,128)(2,1)S(1)}, bf16[8,4096]{1,0:T(8,128)(2,1)}, u32[]{:S(2)}) copy-start(bf16[8,4096]{1,0:T(8,128)(2,1)} %param.14) | copy-start | bytes 196612
  7.9 1.0 %copy-start.3 = (bf16[8,384]{1,0:T(8,128)(2,1)S(1)}, bf16[8,384]{1,0:T(8,128)(2,1)}, u32[]{:S(2)}) copy-start(bf16[8,384]{1,0:T(8,128)(2,1)} %param.15) | copy-start | bytes 18436
  7.9 1.4 %copy-start.7 = (s32[2,8]{1,0:T(2,128)S(1)}, s32[2,8]{1,0:T(2,128)}, u32[]{:S(2)}) copy-start(s32[2,8]{1,0:T(2,128)} %param.18) | copy-start | bytes 196
  7.9 1.5 %copy-start.6 = (f32[2,36]{1,0:T(2,128)S(1)}, f32[2,36]{1,0:T(2,128)}, u32[]{:S(2)}) copy-start(f32[2,36]{1,0:T(2,128)} %param.19) | copy-start | bytes 868
  7.9 1.8 %copy-start.2 = (f32[2,8,36]{2,1,0:T(8,128)S(1)}, f32[2,8,36]{2,1,0:T(8,128)}, u32[]{:S(2)}) copy-start(f32[2,8,36]{2,1,0:T(8,128)} %param.17) | copy-start | bytes 6916
  7.9 2.2 %copy-start.5 = (s32[1,4,8]{2,1,0:T(4,128)S(1)}, s32[1,4,8]{2,1,0:T(4,128)}, u32[]{:S(2)}) copy-start(s32[1,4,8]{2,1,0:T(4,128)} %param.13) | copy-start | bytes 388
  7.9 2.2 %copy-start.4 = (s32[8,8]{1,0:T(8,128)S(1)}, s32[8,8]{1,0:T(8,128)}, u32[]{:S(2)}) copy-start(s32[8,8]{1,0:T(8,128)} %param.12) | copy-start | bytes 772
  7.9 2.2 %copy-start = (s32[8]{0:T(128)S(1)}, s32[8]{0:T(128)}, u32[]{:S(2)}) copy-start(s32[8]{0:T(128)} %agg.1) | copy-start | bytes 100
where the time goes:
time: 74.7 us; the launch traced here: 74.5 us
  Pallas kernels  62.4 us (84%)
  local copies, waits for them, and re-layouts  11.1 us (15%)
  between operations  0.86 us (1%)
    pallas_call x1, Pallas kernels, fused_cycle(): pl.pallas_call(functools.partial(cycle_kernel, n_sec, n_dom), out_shape=(...  62.4 us
    reshape x3, local copies, waits for them, and re-layouts, fused_cycle(): fine_blocks.reshape(8, K, B, B).transpose(0, 2, 1, 3).reshape(8 * B, K * B)  6.39 us

commit v1 on v0

--- a/solution.py
+++ b/solution.py
@@ -31,9 +31,9 @@
     n_sec, n_dom,
     rhs, fine, smooth, restrict, prolong, coarse_own, lists_own, columns, agg,
     x_out, w_out,
-    a_high, a_low, fields, halo, turned, gathered, slots,
-    lists_in, lists_scalar, tiles_in, tiles3, dense, dense_high, dense_low, inverse,
-    coarse_in, state,
+    a_plain, a_high, a_low, fields, halo, turned, gathered, slots,
+    lists_in, lists_scalar, tiles_in, tiles3, dense, dense_high, dense_low, inverse_high, inverse_low,
+    coarse_in, front, total,
     halo_send, halo_recv, list_send, list_recv, list_local,
     tile_send, tile_recv, coarse_send, coarse_recv,
 ):
@@ -114,9 +114,6 @@
         pltpu.make_async_copy(part, part, sem).wait()
 
     first = [relax(half, rhs[half * B:(half + 1) * B, :]) for half in range(2)]
-    high, low = split2(fine[...])
-    a_high[...] = high
-    a_low[...] = low
     dense[...] = jnp.zeros_like(dense)
     turned[40:44] = jnp.zeros((4, B, 128), jnp.float32)
     for q in range(4):
@@ -132,6 +129,18 @@
     publish(0, first)
     tiles_in[me] = coarse_own[...]
     to_others(lambda where: spread_copy(coarse_own, tiles_in, tile_send, tile_recv, where).start())
+    for n in range(8):
+        split_rows = fine[n].reshape(K, B // 2, 128)
+        for pair in range(K // 2):
+            one, two = split_rows[2 * pair], split_rows[2 * pair + 1]
+            even = jnp.where(lane < B, one, pltpu.roll(two, B, 1))
+            odd = jnp.where(lane < B, pltpu.roll(one, B, 1), two)
+            a_plain[pair, pl.ds(n * B, B // 2, stride=2), :] = even
+            a_plain[pair, pl.ds(n * B + 1, B // 2, stride=2), :] = odd
+    for pair in range(K // 2):
+        high, low = split2(a_plain[pair])
+        a_high[:, pair * 128:(pair + 1) * 128] = high
+        a_low[:, pair * 128:(pair + 1) * 128] = low
     for q in range(4):
         @pl.when(links[q][2])
         def _():
@@ -152,7 +161,7 @@
 
     lax.fori_loop(0, 8 * K, find_slot, 0)
 
-    def residual(turn):
+    def residual(turn, exact):
         for q in range(4):
             @pl.when(links[q][2])
             def _():
@@ -168,13 +177,14 @@
                 gathered[half, k * B:(k + 1) * B, 128:256] = low
             span = slice(half * HALF, (half + 1) * HALF)
             both = jnp.dot(a_high[span, :], gathered[half], preferred_element_type=jnp.float32)
-            rest = jnp.dot(a_low[span, :], gathered[half, :, 0:128], preferred_element_type=jnp.float32)
-            product = both[:, 0:128] + both[:, 128:256] + rest
+            product = both[:, 0:128] + both[:, 128:256]
+            if exact:
+                product += jnp.dot(a_low[span, :], gathered[half, :, 0:128], preferred_element_type=jnp.float32)
             result.append(rhs[half * B:(half + 1) * B, :] - diagonal(product))
         return result
 
-    def sweep(turn):
-        left = residual(turn)
+    def sweep(turn, exact):
+        left = residual(turn, exact)
         return [fields[turn, half * B:(half + 1) * B, :] + relax(half, left[half]) for half in range(2)]
 
     position = lax.broadcasted_iota(jnp.int32, (1, 2 * rows), 1)
@@ -195,8 +205,27 @@
                 cut = slice(v * 128, (v + 1) * 128)
                 dense[a * rows:(a + 1) * rows, cut] += jnp.where(names == named[:, cut], spread, 0.0)
 
+    def three_terms(high, low, right_high, right_low):
+        both = jnp.dot(jnp.concatenate([high, low], axis=0), right_high, preferred_element_type=jnp.float32)
+        rest = jnp.dot(high, right_low, preferred_element_type=jnp.float32)
+        return both[0:16] + both[16:32] + rest
+
+    def smoothed_front():
+        high, low = split2(front[...])
+        parts = []
+        for a in range(NAGG):
+            cut = slice(a * rows, (a + 1) * rows)
+            parts.append(three_terms(high[:, cut], low[:, cut], inverse_high[a], inverse_low[a]))
+        return jnp.concatenate(parts, axis=1)
+
+    def grow():
+        moved = smoothed_front()
+        total[...] += moved
+        high, low = split2(moved)
+        front[...] -= three_terms(high, low, dense_high[...], dense_low[...])
+
     def pre_turn(turn, carry):
-        publish(turn + 1, sweep(turn))
+        publish(turn + 1, sweep(turn, True))
 
         @pl.when(turn == 0)
         def _():
@@ -207,15 +236,41 @@
             tiles3[:, 128:256] = low
             tiles3[:, 256:384] = (whole - high.astype(jnp.float32) - low.astype(jnp.float32)).astype(jnp.bfloat16)
 
-        add_blocks(2 * turn)
-        add_blocks(2 * turn + 1)
+        @pl.when(turn < 2)
+        def _():
+            for i in range(3):
+                add_blocks(3 * turn + i)
+
+        @pl.when(turn == 2)
+        def _():
+            add_blocks(6)
+            add_blocks(7)
+            row_part = lax.broadcasted_iota(jnp.int32, (rows, 1), 0) // 8
+            for a in range(NAGG):
+                spread = pick((a * KC + lax.rem(to_lane, 8)) * 8 + BC)
+                for v in range(rows // 128):
+                    column_part = (lane + v * 128) // 8
+                    high, low = split2(jnp.where(row_part == column_part, spread, 0.0))
+                    inverse_high[a, :, v * 128:(v + 1) * 128] = high
+                    inverse_low[a, :, v * 128:(v + 1) * 128] = low
+            high, low = split2(dense[...])
+            dense_high[...] = high
+            dense_low[...] = low
+            index = lax.broadcasted_iota(jnp.int32, (2 * 8, 1), 0)
+            wanted = index // 8 * rows + me * 8 + lax.rem(index, 8)
+            front[...] = jnp.where((wanted == position) & (lax.rem(index, 8) < BC), 1.0, 0.0)
+            total[...] = jnp.zeros_like(total)
+
+        @pl.when(turn == 3)
+        def _():
+            grow()
+            grow()
+
         return carry
 
     lax.fori_loop(0, NPRE - 1, pre_turn, 0)
-    for j in range(BC):
-        inverse[j] = pick((to_lane // R * KC + j) * 8 + BC)
-
-    left = residual(NPRE - 1)
+
+    left = residual(NPRE - 1, True)
     sums = [jnp.zeros((8, 128), jnp.float32) for _ in range(NAGG)]
     for half in range(2):
         terms = jnp.dot(
@@ -233,41 +288,21 @@
     folded = [fold(value) for value in sums]
     coarse_in[me] = jnp.where(group == 0, folded[0], jnp.where(group == 1, folded[1], 0.0))
     to_others(lambda where: spread_copy(coarse_in.at[me], coarse_in, coarse_send, coarse_recv, where).start())
-    high, low = split2(dense[...])
-    dense_high[...] = high
-    dense_low[...] = low
+    for _ in range(CITERS - 2):
+        grow()
+    solve = total[...] + smoothed_front()
+    solve_high, solve_low = split2(solve)
     wait_bytes(coarse_in, coarse_recv)
-    right = coarse_in[...].reshape(rows, 128)
-
-    def precond(value):
-        tiles = value.reshape(count, 8, 128)
-        total = jnp.zeros((rows, 128), jnp.float32)
-        for j in range(BC):
-            total = total + inverse[j] * jnp.broadcast_to(tiles[:, j:j + 1, :], (count, 8, 128)).reshape(rows, 128)
-        return total
-
-    def coarse_turn(step, carry):
-        value = state[...]
-        value_r, value_l = pltpu.roll(value, R, 1), pltpu.roll(value, 128 - R, 1)
-        stacked = jnp.concatenate(
-            [jnp.where(group == 0, value, value_r), jnp.where(group == 0, value_l, value)], axis=0
-        )
-        high, low = split2(stacked)
-        both = jnp.dot(dense_high[...], jnp.concatenate([high, low], axis=1), preferred_element_type=jnp.float32)
-        rest = jnp.dot(dense_low[...], high, preferred_element_type=jnp.float32)
-        product = both[:, 0:128] + both[:, 128:256] + rest
-        applied = jnp.where(group == 0, product[0:rows], product[rows:2 * rows])
-        inside = lax.rem(lax.broadcasted_iota(jnp.int32, (rows, 1), 0), 8) < BC
-        state[...] = value + precond(jnp.where(inside & (group < NAGG), right - applied, 0.0))
-        return carry
-
-    state[...] = precond(right)
-    lax.fori_loop(0, CITERS, coarse_turn, 0)
-    own = state[pl.ds(pl.multiple_of(me * 8, 8), 8), :]
-    w_out[...] = own
-    answers = [
-        fold(jnp.where(group == a, own, 0.0)) for a in range(NAGG)
+    right_high, right_low = split2(coarse_in[...].reshape(rows, 128))
+    pieces = [
+        three_terms(
+            solve_high[:, a * rows:(a + 1) * rows], solve_low[:, a * rows:(a + 1) * rows], right_high, right_low
+        )
+        for a in range(NAGG)
     ]
+    own = jnp.where(group == 0, pieces[0] + pltpu.roll(pieces[1], 128 - R, 1), 0.0)
+    answers = [fold(own[a * 8:(a + 1) * 8]) for a in range(NAGG)]
+    w_out[...] = jnp.where(group == 0, answers[0], answers[1])
     corrected = []
     for half in range(2):
         picked = jnp.zeros((8, 128), jnp.float32)
@@ -282,11 +317,11 @@
     publish(NPRE, corrected)
 
     def post_turn(turn, carry):
-        publish(turn + 1, sweep(turn))
+        publish(turn + 1, sweep(turn, False))
         return carry
 
     lax.fori_loop(NPRE, TURNS - 1, post_turn, 0)
-    last = sweep(TURNS - 1)
+    last = sweep(TURNS - 1, False)
     for half in range(2):
         x_out[half * B:(half + 1) * B, :] = last[half]
 
@@ -311,7 +346,6 @@
     count = n_sec * n_dom
     rows = 8 * count
     packed = rhs.reshape(2, 4, B, R).transpose(0, 2, 1, 3).reshape(2 * B, 4 * R)
-    fine = fine_blocks.reshape(8, K, B, B).transpose(0, 2, 1, 3).reshape(8 * B, K * B)
     smooth = smoother.reshape(8 * B, B)
     tiles = jnp.pad(prolong.reshape(8, B, BC), ((0, 0), (0, 0), (0, 2)))
     restrict = tiles.transpose(0, 2, 1).reshape(64, B)
@@ -333,6 +367,7 @@
         in_specs=[vmem] * 7 + [smem] * 2,
         out_specs=(vmem, vmem),
         scratch_shapes=[
+            pltpu.VMEM((4, 512, 128), f32),
             pltpu.VMEM((512, 512), bf16),
             pltpu.VMEM((512, 512), bf16),
             pltpu.VMEM((TURNS, 128, 128), f32),
@@ -347,9 +382,11 @@
             pltpu.VMEM((2 * rows, 2 * rows), f32),
             pltpu.VMEM((2 * rows, 2 * rows), bf16),
             pltpu.VMEM((2 * rows, 2 * rows), bf16),
-            pltpu.VMEM((BC, rows, 128), f32),
+            pltpu.VMEM((NAGG, rows, rows), bf16),
+            pltpu.VMEM((NAGG, rows, rows), bf16),
             pltpu.VMEM((count, 8, 128), f32),
-            pltpu.VMEM((rows, 128), f32),
+            pltpu.VMEM((16, 2 * rows), f32),
+            pltpu.VMEM((16, 2 * rows), f32),
             pltpu.SemaphoreType.DMA((TURNS, 4)),
             pltpu.SemaphoreType.DMA((TURNS, 4)),
             pltpu.SemaphoreType.DMA((4,)),
@@ -363,7 +400,7 @@
         compiler_params=pltpu.CompilerParams(
             collective_id=0, has_side_effects=True, vmem_limit_bytes=48 * 1024 * 1024
         ),
-    )(packed, fine, smooth, restrict, lifts, coarse_own, lists, fine_columns.reshape(64), agg_map)
+    )(packed, fine_blocks, smooth, restrict, lifts, coarse_own, lists, fine_columns.reshape(64), agg_map)
     solved = x.reshape(2, B, 4, R).transpose(0, 2, 1, 3).reshape(8, B * R)
     coarse = w[:BC, :NAGG * R].reshape(BC, NAGG, R).transpose(1, 0, 2).reshape(NAGG, BC * R)
     return solved, coarse

time: 74.7 us -> 70.1 us (0.938)
  local copies, waits for them, and re-layouts: 11.1 us -> 8.65 us
  Pallas kernels: 62.4 us -> 60.2 us
    reshape x3 -> x0, local copies, waits for them, and re-layouts: 6.39 us -> none  [fused_cycle(): fine_blocks.reshape(8, K, B, B).transpose(0, 2, 1, 3).reshape(8 * B, K * B)]
    unnamed x16 -> x18, local copies, waits for them, and re-layouts: 0.3 us -> 4.41 us
    pallas_call x1, Pallas kernels: 62.4 us -> 60.2 us  [fused_cycle(): pl.pallas_call(functools.partial(cycle_kernel, n_sec, n_dom), out_shape=(...]
    reshape x3, local copies, waits for them, and re-layouts: 1.18 us -> 0.33 us  [fused_cycle(): packed = rhs.reshape(2, 4, B, R).transpose(0, 2, 1, 3).reshape(2 * B, 4 * R)]
where the time goes in v1:
time: 70.1 us; the launch traced here: 69.7 us
  Pallas kernels  60.2 us (86%)
  local copies, waits for them, and re-layouts  8.65 us (12%)
  between operations  0.77 us (1%)
    pallas_call x1, Pallas kernels, fused_cycle(): pl.pallas_call(functools.partial(cycle_kernel, n_sec, n_dom), out_shape=(...  60.2 us
    unnamed x18, local copies, waits for them, and re-layouts  4.41 us

profile of v1, /device:TPU:0, one launch (start us, length us, event | category | flops | bytes accessed | tf_op | source)
XLA Modules:
  0.0 69.7 jit_solution(6791018673330077493)
XLA Ops:
  0.6 0.9 %reshape.52 = bf16[8,64,6]{2,1,0:T(8,128)(2,1)S(1)} reshape(bf16[8,384]{1,0:T(8,128)(2,1)} %param.15) | data formatting | bytes 12288 | tf_op jit(solution)/shard_map/reshape | solution.py:350
  1.7 0.1 copy.20
  1.8 0.7 copy-done.2
  2.5 0.1 reshape.49
  2.6 0.1 copy.19
  2.7 0.1 reshape.50
  2.8 0.1 copy.24.rhs
  2.9 0.6 copy-done.7
  3.6 0.2 copy.22
  3.8 0.5 copy-done.4
  4.4 0.6 copy-done.8
  5.1 0.1 fusion
  5.3 0.1 reshape.56.coarse_own
  5.4 0.7 %copy-done.3 = bf16[8,4096]{1,0:T(8,128)(2,1)S(1)} copy-done((bf16[8,4096]{1,0:T(8,128)(2,1)S(1)}, bf16[8,4096]{1,0:T(8,128)(2,1)}, u32[]{:S(2)}) %copy-start.3) | copy-done | bytes 65560
  6.1 0.2 reshape.51.smooth
  6.3 0.5 copy-done.6
  6.8 0.2 copy-done.5
  7.1 0.6 copy-done.1
  7.6 60.2 %shard_map.113 = (f32[128,128]{1,0:T(8,128)S(1)}, f32[8,128]{1,0:T(8,128)S(1)}) custom-call(f32[128,128]{1,0:T(8,128)S(1)} %copy.24.rhs, f32[8,8,4096]{2,1,0:T(8,128)S(1)} %copy-done, bf16[512,64]{1,0:T(8,128)(2,1)S(1)} %reshape.51.smooth, bf16[64,64]{1,0:T(8,128)(2,1)S(1)} %bitcast.26, f32[512,8]{1,0:T(8,128)S(1)} %bitcast_convert_fusion.prolong, ...), custom_call_target="tpu_custom_call" | custom-call | tf_op jit(solution)/shard_map/pallas_call | solution.py:364
  67.8 0.1 copy.25
  67.9 0.1 reshape.58
  68.1 0.1 copy.26
  68.2 0.8 %reshape.59 = f32[8,2048]{1,0:T(8,128)} reshape(f32[2,4,64,32]{3,2,1,0:T(8,128)S(1)} %copy.26) | data formatting | bytes 131072 | tf_op jit(solution)/shard_map/reshape | solution.py:404
  69.1 0.7 reshape.61
  (24 shorter events, 0.6 us)
Async XLA Ops:
  1.6 0.8 %copy-start.2 = (f32[8,2048]{1,0:T(8,128)S(1)}, f32[8,2048]{1,0:T(8,128)}, u32[]{:S(2)}) copy-start(f32[8,2048]{1,0:T(8,128)} %param.10) | copy-start | bytes 196612
  1.7 5.4 %copy-start = (f32[8,8,4096]{2,1,0:T(8,128)S(1)}, f32[8,8,4096]{2,1,0:T(8,128)}, u32[]{:S(2)}) copy-start(f32[8,8,4096]{2,1,0:T(8,128)} %fine.1) | copy-start | bytes 3145732
  2.8 0.7 copy-start.7
  3.6 0.7 %copy-start.4 = (f32[2,8,36]{2,1,0:T(8,128)S(1)}, f32[2,8,36]{2,1,0:T(8,128)}, u32[]{:S(2)}) copy-start(f32[2,8,36]{2,1,0:T(8,128)} %param.17) | copy-start | bytes 6916
  4.3 0.7 copy-start.8
  5.3 0.8 %copy-start.3 = (bf16[8,4096]{1,0:T(8,128)(2,1)S(1)}, bf16[8,4096]{1,0:T(8,128)(2,1)}, u32[]{:S(2)}) copy-start(bf16[8,4096]{1,0:T(8,128)(2,1)} %param.14) | copy-start | bytes 196612
  6.1 0.7 copy-start.6
  6.3 0.7 copy-start.5
  7.0 0.7 copy-start.1

commit v2 on v1

--- a/solution.py
+++ b/solution.py
@@ -71,10 +71,10 @@
         )
         return diagonal(product)
 
-    def halo_copy(turn, q):
+    def halo_copy(turn, q, half):
         return pltpu.make_async_remote_copy(
-            src_ref=fields.at[turn], dst_ref=halo.at[turn, q],
-            send_sem=halo_send.at[turn, q], recv_sem=halo_recv.at[turn, q],
+            src_ref=fields.at[turn, half], dst_ref=halo.at[turn, q, half],
+            send_sem=halo_send.at[turn, q, half], recv_sem=halo_recv.at[turn, q, half],
             device_id=links[q][0], device_id_type=MESH,
         )
 
@@ -85,23 +85,19 @@
             device_id=links[q][0], device_id_type=MESH,
         )
 
-    def turn_tiles(value, source):
+    def turn_tiles(part, source, half):
+        for step in range(4):
+            turned[(source * 2 + half) * 4 + step] = part if step == 0 else pltpu.roll(part, step * R, 1)
+
+    def publish(turn, make_half):
         for half in range(2):
-            part = value[half * B:(half + 1) * B, :]
-            for step in range(4):
-                turned[(source * 2 + half) * 4 + step] = part if step == 0 else pltpu.roll(part, step * R, 1)
-
-    def start_halo(turn):
-        for q in range(4):
-            @pl.when(links[q][1])
-            def _():
-                halo_copy(turn, q).start()
-
-    def publish(turn, halves):
+            fields[turn, half] = make_half(half)
+            for q in (2, 3, 0, 1):
+                @pl.when(links[q][1])
+                def _():
+                    halo_copy(turn, q, half).start()
         for half in range(2):
-            fields[turn, half * B:(half + 1) * B, :] = halves[half]
-        start_halo(turn)
-        turn_tiles(fields[turn], 0)
+            turn_tiles(fields[turn, half], 0, half)
 
     def spread_copy(source, place, send_sem, recv_sem, where):
         return pltpu.make_async_remote_copy(
@@ -126,7 +122,7 @@
         @pl.when(links[q][1])
         def _():
             list_copy(q).start()
-    publish(0, first)
+    publish(0, lambda half: first[half])
     tiles_in[me] = coarse_own[...]
     to_others(lambda where: spread_copy(coarse_own, tiles_in, tile_send, tile_recv, where).start())
     for n in range(8):
@@ -161,13 +157,13 @@
 
     lax.fori_loop(0, 8 * K, find_slot, 0)
 
-    def residual(turn, exact):
-        for q in range(4):
-            @pl.when(links[q][2])
-            def _():
-                halo_copy(turn, q).wait_recv()
-                turn_tiles(halo[turn, q], q + 1)
-        result = []
+    def gather(turn):
+        for half in range(2):
+            for q in range(4):
+                @pl.when(links[q][2])
+                def _():
+                    halo_copy(turn, q, half).wait_recv()
+                    turn_tiles(halo[turn, q, half], q + 1, half)
         for half in range(2):
             for k in range(K):
                 t = [turned[slots[(half * 4 + g) * K + k]] for g in range(4)]
@@ -175,17 +171,18 @@
                 high, low = split2(tile)
                 gathered[half, k * B:(k + 1) * B, 0:128] = high
                 gathered[half, k * B:(k + 1) * B, 128:256] = low
-            span = slice(half * HALF, (half + 1) * HALF)
-            both = jnp.dot(a_high[span, :], gathered[half], preferred_element_type=jnp.float32)
-            product = both[:, 0:128] + both[:, 128:256]
-            if exact:
-                product += jnp.dot(a_low[span, :], gathered[half, :, 0:128], preferred_element_type=jnp.float32)
-            result.append(rhs[half * B:(half + 1) * B, :] - diagonal(product))
-        return result
+
+    def residual(half, exact):
+        span = slice(half * HALF, (half + 1) * HALF)
+        both = jnp.dot(a_high[span, :], gathered[half], preferred_element_type=jnp.float32)
+        product = both[:, 0:128] + both[:, 128:256]
+        if exact:
+            product += jnp.dot(a_low[span, :], gathered[half, :, 0:128], preferred_element_type=jnp.float32)
+        return rhs[half * B:(half + 1) * B, :] - diagonal(product)
 
     def sweep(turn, exact):
-        left = residual(turn, exact)
-        return [fields[turn, half * B:(half + 1) * B, :] + relax(half, left[half]) for half in range(2)]
+        gather(turn)
+        return lambda half: fields[turn, half] + relax(half, residual(half, exact))
 
     position = lax.broadcasted_iota(jnp.int32, (1, 2 * rows), 1)
     within = lax.rem(position, rows)
@@ -270,7 +267,8 @@
 
     lax.fori_loop(0, NPRE - 1, pre_turn, 0)
 
-    left = residual(NPRE - 1, True)
+    gather(NPRE - 1)
+    left = [residual(half, True) for half in range(2)]
     sums = [jnp.zeros((8, 128), jnp.float32) for _ in range(NAGG)]
     for half in range(2):
         terms = jnp.dot(
@@ -313,8 +311,8 @@
             prolong[half * HALF:(half + 1) * HALF, :], picked,
             precision=lax.Precision.HIGHEST, preferred_element_type=jnp.float32,
         )
-        corrected.append(fields[NPRE - 1, half * B:(half + 1) * B, :] + diagonal(product))
-    publish(NPRE, corrected)
+        corrected.append(fields[NPRE - 1, half] + diagonal(product))
+    publish(NPRE, lambda half: corrected[half])
 
     def post_turn(turn, carry):
         publish(turn + 1, sweep(turn, False))
@@ -323,13 +321,14 @@
     lax.fori_loop(NPRE, TURNS - 1, post_turn, 0)
     last = sweep(TURNS - 1, False)
     for half in range(2):
-        x_out[half * B:(half + 1) * B, :] = last[half]
+        x_out[half * B:(half + 1) * B, :] = last(half)
 
     def drain(turn, carry):
         for q in range(4):
             @pl.when(links[q][1])
             def _():
-                halo_copy(turn, q).wait_send()
+                for half in range(2):
+                    halo_copy(turn, q, half).wait_send()
         return carry
 
     lax.fori_loop(0, TURNS, drain, 0)
@@ -370,8 +369,8 @@
             pltpu.VMEM((4, 512, 128), f32),
             pltpu.VMEM((512, 512), bf16),
             pltpu.VMEM((512, 512), bf16),
-            pltpu.VMEM((TURNS, 128, 128), f32),
-            pltpu.VMEM((TURNS, 4, 128, 128), f32),
+            pltpu.VMEM((TURNS, 2, B, 128), f32),
+            pltpu.VMEM((TURNS, 4, 2, B, 128), f32),
             pltpu.VMEM((44, B, 128), f32),
             pltpu.VMEM((2, 512, 256), bf16),
             pltpu.SMEM((64,), jnp.int32),
@@ -387,8 +386,8 @@
             pltpu.VMEM((count, 8, 128), f32),
             pltpu.VMEM((16, 2 * rows), f32),
             pltpu.VMEM((16, 2 * rows), f32),
-            pltpu.SemaphoreType.DMA((TURNS, 4)),
-            pltpu.SemaphoreType.DMA((TURNS, 4)),
+            pltpu.SemaphoreType.DMA((TURNS, 4, 2)),
+            pltpu.SemaphoreType.DMA((TURNS, 4, 2)),
             pltpu.SemaphoreType.DMA((4,)),
             pltpu.SemaphoreType.DMA((4,)),
             pltpu.SemaphoreType.DMA,

time: 70.1 us -> 69.9 us (level)
  no operation moved by 1% of the time
where the time goes in v2:
time: 69.9 us; the launch traced here: 69.6 us
  Pallas kernels  60 us (86%)
  local copies, waits for them, and re-layouts  8.65 us (12%)
  between operations  0.77 us (1%)
    pallas_call x1, Pallas kernels, fused_cycle(): pl.pallas_call(functools.partial(cycle_kernel, n_sec, n_dom), out_shape=(...  60 us
    unnamed x18, local copies, waits for them, and re-layouts  4.41 us

profile of v2, /device:TPU:0, one launch (start us, length us, event | category | flops | bytes accessed | tf_op | source)
XLA Modules:
  0.0 69.6 jit_solution(10408434647930595378)
XLA Ops:
  0.6 0.9 %reshape.52 = bf16[8,64,6]{2,1,0:T(8,128)(2,1)S(1)} reshape(bf16[8,384]{1,0:T(8,128)(2,1)} %param.15) | data formatting | bytes 12288 | tf_op jit(solution)/shard_map/reshape | solution.py:349
  1.7 0.1 copy.20
  1.8 0.7 copy-done.2
  2.5 0.1 reshape.49
  2.6 0.1 copy.19
  2.7 0.1 reshape.50
  2.8 0.1 copy.24.rhs
  2.9 0.6 copy-done.7
  3.6 0.2 copy.22
  3.8 0.5 copy-done.4
  4.4 0.6 copy-done.8
  5.1 0.1 fusion
  5.3 0.1 reshape.56.coarse_own
  5.4 0.7 %copy-done.3 = bf16[8,4096]{1,0:T(8,128)(2,1)S(1)} copy-done((bf16[8,4096]{1,0:T(8,128)(2,1)S(1)}, bf16[8,4096]{1,0:T(8,128)(2,1)}, u32[]{:S(2)}) %copy-start.3) | copy-done | bytes 65560
  6.1 0.2 reshape.51.smooth
  6.3 0.5 copy-done.6
  6.8 0.2 copy-done.5
  7.1 0.6 copy-done.1
  7.6 60.0 %shard_map.113 = (f32[128,128]{1,0:T(8,128)S(1)}, f32[8,128]{1,0:T(8,128)S(1)}) custom-call(f32[128,128]{1,0:T(8,128)S(1)} %copy.24.rhs, f32[8,8,4096]{2,1,0:T(8,128)S(1)} %copy-done, bf16[512,64]{1,0:T(8,128)(2,1)S(1)} %reshape.51.smooth, bf16[64,64]{1,0:T(8,128)(2,1)S(1)} %bitcast.26, f32[512,8]{1,0:T(8,128)S(1)} %bitcast_convert_fusion.prolong, ...), custom_call_target="tpu_custom_call" | custom-call | tf_op jit(solution)/shard_map/pallas_call | solution.py:363
  67.7 0.1 copy.25
  67.8 0.1 reshape.58
  67.9 0.1 copy.26
  68.1 0.8 %reshape.59 = f32[8,2048]{1,0:T(8,128)} reshape(f32[2,4,64,32]{3,2,1,0:T(8,128)S(1)} %copy.26) | data formatting | bytes 131072 | tf_op jit(solution)/shard_map/reshape | solution.py:403
  68.9 0.7 reshape.61
  (24 shorter events, 0.6 us)
Async XLA Ops:
  1.6 0.8 %copy-start.2 = (f32[8,2048]{1,0:T(8,128)S(1)}, f32[8,2048]{1,0:T(8,128)}, u32[]{:S(2)}) copy-start(f32[8,2048]{1,0:T(8,128)} %param.10) | copy-start | bytes 196612
  1.7 5.4 %copy-start = (f32[8,8,4096]{2,1,0:T(8,128)S(1)}, f32[8,8,4096]{2,1,0:T(8,128)}, u32[]{:S(2)}) copy-start(f32[8,8,4096]{2,1,0:T(8,128)} %fine.1) | copy-start | bytes 3145732
  2.8 0.7 copy-start.7
  3.6 0.7 %copy-start.4 = (f32[2,8,36]{2,1,0:T(8,128)S(1)}, f32[2,8,36]{2,1,0:T(8,128)}, u32[]{:S(2)}) copy-start(f32[2,8,36]{2,1,0:T(8,128)} %param.17) | copy-start | bytes 6916
  4.3 0.7 copy-start.8
  5.3 0.8 %copy-start.3 = (bf16[8,4096]{1,0:T(8,128)(2,1)S(1)}, bf16[8,4096]{1,0:T(8,128)(2,1)}, u32[]{:S(2)}) copy-start(bf16[8,4096]{1,0:T(8,128)(2,1)} %param.14) | copy-start | bytes 196612
  6.1 0.7 copy-start.6
  6.3 0.7 copy-start.5
  7.0 0.7 copy-start.1
